TPU v7x, 512 devices: a whole 4x8x8 slice. The times are simulated.
512 devices in a mesh: ens: 4 (over y_hi), lat: 8 (over y_lo, x), lon: 16 (over z, core).
Axes of the slice: x: 4, y: 8 (y_hi: 4, y_lo: 2; y = y_hi * 2 + y_lo), z: 8, core: 2. Of those that a mesh axis runs over, the one named last changes fastest.
Arguments:
- initial_state: float32 [24, 128, 2048], P('ens', 'lat', 'lon'), parts along dimension 0, may hold values from -6 to 6
- diffusion: float32 [128, 2048], P('lat', 'lon'), may hold values from 0.05 to 0.2
- mixing: float32 [6, 6], replicated, may hold values from -0.3 to 0.3
- land_mask: int32 [128, 2048], P('lat', 'lon'), may hold values 0 or 1
- first_layer: bfloat16 [128, 54], replicated, may hold values from -0.875 to 0.875
- second_layer: bfloat16 [128, 128], replicated, may hold values from -0.5 to 0.5
- output_layer: bfloat16 [6, 128], replicated, may hold values from -0.5 to 0.5
- cotangent: float32 [24, 128, 2048], P('ens', 'lat', 'lon'), parts along dimension 0, may hold values from -20 to 20
- update_noise: float32 [96256], P('ens'), parts along dimension 0, may hold values from -0.15 to 0.15
Outputs:
- final_state: float32 [24, 128, 2048], P('ens', 'lat', 'lon'), parts along dimension 0
- initial_adjoint: float32 [24, 128, 2048], P('ens', 'lat', 'lon'), parts along dimension 0
- new_params: float32 [96256], P('ens'), parts along dimension 0
- noise_ratio: float32 [4], P('ens'), parts along dimension 0
There are 4 independent parts, one for each index of `ens`. A program takes and returns all parts, laid end to end along the dimension named above; an argument that names none is the same for every part. Nothing has to cross between parts.
All inputs are finite; a program needn't handle non-finite values. No bound on the sum of `land_mask` on one device may be relied on, other than what follows from the above.
Results may differ from a plain program's by a relative error of at most 0.0033.
Values sent between devices are 32-bit elements; how exact they have to be, the bound alone decides.
A program may use at most 64 MiB of HBM per device.

v0:
```python
import jax
import jax.numpy as jnp
from jax import lax
from jax.sharding import PartitionSpec as P

STEPS = 2
closure_dt = 0.1
learn_rate = 0.1
epsilon = 1e-06
offsets = [(row_shift, col_shift) for row_shift in (-1, 0, 1) for col_shift in (-1, 0, 1)]


def with_halo(value, sides, width, wrap):
    for axis, dim in sides:
        devices, length = (lax.axis_size(axis), value.shape[dim])
        up = [(i, (i + 1) % devices) for i in range(devices if wrap else devices - 1)]
        down = [(j, i) for i, j in up]
        last = lax.slice_in_dim(value, length - width, length, axis=dim)
        first = lax.slice_in_dim(value, 0, width, axis=dim)
        before = lax.ppermute(last, axis, up)
        after = lax.ppermute(first, axis, down)
        value = jnp.concatenate([before, value, after], axis=dim)
    return value


def contract_last(left, right):
    return lax.dot_general(
        left, right, (((1,), (1,)), ((), ())), preferred_element_type=jnp.float32
    )


def contract_first(left, right):
    return lax.dot_general(
        left, right, (((0,), (0,)), ((), ())), preferred_element_type=jnp.float32
    )


def build_patch(slab, rows, cols):
    return jnp.concatenate(
        [
            slab[:, 1 + row_shift : 1 + row_shift + rows, 1 + col_shift : 1 + col_shift + cols]
            for row_shift, col_shift in offsets
        ],
        axis=0,
    )


def hidden_layers(flat, first_layer, second_layer):
    hidden_one = jnp.tanh(jnp.dot(first_layer, flat, preferred_element_type=jnp.float32)).astype(
        jnp.bfloat16
    )
    hidden_two = jnp.tanh(
        jnp.dot(second_layer, hidden_one, preferred_element_type=jnp.float32)
    ).astype(jnp.bfloat16)
    return (hidden_one, hidden_two)


def forward_block(slab, mask_rows, diff_rows, mixing, first_layer, second_layer, output_layer):
    fields = slab.shape[0]
    rows = slab.shape[1] - 2
    cols = slab.shape[2] - 2
    count = rows * cols
    patch = build_patch(slab, rows, cols)
    centre = patch[4 * fields : 5 * fields]
    laplace = (
        patch[fields : 2 * fields]
        + patch[3 * fields : 4 * fields]
        + patch[5 * fields : 6 * fields]
        + patch[7 * fields : 8 * fields]
        - 4.0 * centre
    )
    flat = patch.reshape(9 * fields, count).astype(jnp.bfloat16)
    hidden_one, hidden_two = hidden_layers(flat, first_layer, second_layer)
    tendency = jnp.dot(output_layer, hidden_two, preferred_element_type=jnp.float32)
    mixed = jnp.dot(mixing, centre.reshape(fields, count), precision=lax.Precision.HIGHEST)
    update = (
        centre
        + diff_rows[None] * laplace
        + (mixed + closure_dt * tendency).reshape(fields, rows, cols)
    )
    return mask_rows[None] * update


def backward_block(
    slab, adjoint_rows, mask_rows, diff_rows, mixing, first_layer, second_layer, output_layer
):
    fields = slab.shape[0]
    rows = slab.shape[1] - 2
    cols = slab.shape[2] - 2
    count = rows * cols
    patch = build_patch(slab, rows, cols)
    flat = patch.reshape(9 * fields, count).astype(jnp.bfloat16)
    hidden_one, hidden_two = hidden_layers(flat, first_layer, second_layer)
    masked = (mask_rows[None] * adjoint_rows).reshape(fields, count)
    out_grad = (closure_dt * masked).astype(jnp.bfloat16)
    back_two = (
        contract_first(output_layer, out_grad) * (1.0 - jnp.square(hidden_two.astype(jnp.float32)))
    ).astype(jnp.bfloat16)
    back_one = (
        contract_first(second_layer, back_two) * (1.0 - jnp.square(hidden_one.astype(jnp.float32)))
    ).astype(jnp.bfloat16)
    patch_grad = contract_first(first_layer, back_one)
    direct = masked + lax.dot_general(
        mixing,
        masked,
        (((0,), (0,)), ((), ())),
        precision=lax.Precision.HIGHEST,
        preferred_element_type=jnp.float32,
    )
    spread = diff_rows.reshape(1, count) * masked
    blank = jnp.zeros_like(masked)
    extra = jnp.concatenate(
        [blank, spread, blank, spread, direct - 4.0 * spread, spread, blank, spread, blank], axis=0
    )
    patch_grad = (patch_grad + extra).reshape(9 * fields, rows, cols)
    grads = jnp.concatenate(
        [
            contract_last(back_one, flat).ravel(),
            contract_last(back_two, hidden_one).ravel(),
            contract_last(out_grad, hidden_two).ravel(),
        ]
    )
    return (patch_grad, grads)


def on_device(
    initial_state,
    diffusion,
    mixing,
    land_mask,
    first_layer,
    second_layer,
    output_layer,
    cotangent,
    update_noise,
):
    fields, rows, cols = initial_state.shape
    mask = land_mask.astype(jnp.float32)
    state = initial_state
    saved = []
    for step in range(STEPS):
        wide = with_halo(state, (("lon", 2),), 1, True)
        padded = with_halo(wide, (("lat", 1),), 1, False)
        saved.append(padded)
        state = forward_block(
            padded, mask, diffusion, mixing, first_layer, second_layer, output_layer
        )
    adjoint = cotangent
    local_grad = jnp.zeros((first_layer.size + second_layer.size + output_layer.size,), jnp.float32)
    for step in reversed(range(STEPS)):
        patch_grad, grads = backward_block(
            saved[step], adjoint, mask, diffusion, mixing, first_layer, second_layer, output_layer
        )
        local_grad = local_grad + grads
        wide_grad = with_halo(patch_grad, (("lon", 2),), 1, True)
        grad_pad = with_halo(wide_grad, (("lat", 1),), 1, False)
        total = jnp.zeros((fields, rows, cols), jnp.float32)
        for number, (row_shift, col_shift) in enumerate(offsets):
            total = (
                total
                + grad_pad[
                    number * fields : (number + 1) * fields,
                    1 - row_shift : 1 - row_shift + rows,
                    1 - col_shift : 1 - col_shift + cols,
                ]
            )
        adjoint = total
    params_count = local_grad.shape[0]
    band = lax.psum(local_grad, "lon")
    total_grad, band_square = lax.psum((band, jnp.sum(band * band)), "lat")
    grad_square = jnp.sum(total_grad * total_grad)
    noise_ratio = (band_square / (grad_square + epsilon)).reshape(1)
    params = jnp.concatenate(
        [
            first_layer.astype(jnp.float32).ravel(),
            second_layer.astype(jnp.float32).ravel(),
            output_layer.astype(jnp.float32).ravel(),
        ]
    )
    new_params = (
        params
        - learn_rate * total_grad / jnp.sqrt(grad_square / params_count + epsilon)
        + update_noise
    )
    return (state, adjoint, new_params, noise_ratio)


def solution(mesh):
    placed = (
        P("ens", "lat", "lon"),
        P("lat", "lon"),
        P(),
        P("lat", "lon"),
        P(),
        P(),
        P(),
        P("ens", "lat", "lon"),
        P("ens"),
    )
    return jax.shard_map(
        on_device,
        mesh=mesh,
        in_specs=placed,
        out_specs=(P("ens", "lat", "lon"), P("ens", "lat", "lon"), P("ens"), P("ens")),
        check_vma=False,
    )
```

profile of v0, /device:TPU:40, one launch (start us, length us, event | category | flops | bytes accessed | tf_op | source)
XLA Modules:
  0.0 304.6 jit_solution(4147958158141349705)
XLA Ops:
  8.2 8.5 %collective-permute-start.1 = (f32[6,16,1]{2,1,0:T(8,128)S(1)}, f32[6,16,1]{2,1,0:T(8,128)S(1)}, u32[]{:S(2)}, u32[]{:S(2)}) collective-permute-start(f32[6,16,1]{2,1,0:T(8,128)S(1)} %get-tuple-element.31), channel_id=1, source_target_pairs={{1,0},{2,1},{3,2},{4,3},{5,4},{6,5},{7,6},{8,7},{9,8},{10,9},{11,1... | collective-permute-start | bytes 1160 | tf_op jit(solution)/shard_map/ppermute | solution.py:21
  16.7 1.8 collective-permute-done
  18.6 5.5 %collective-permute-start.3 = (f32[6,1,130]{2,1,0:T(1,128)S(1)}, f32[6,1,130]{2,1,0:T(1,128)S(1)}, u32[]{:S(2)}, u32[]{:S(2)}) collective-permute-start(f32[6,1,130]{2,1,0:T(1,128)S(1)} %get-tuple-element.26), channel_id=1, source_target_pairs={{16,0},{32,16},{48,32},{64,48},{80,64},{96,80},{112,96},{17,1},{33... | collective-permute-start | bytes 9368 | tf_op jit(solution)/shard_map/ppermute | solution.py:21
  24.0 1.9 collective-permute-start.2
  26.7 5.0 %collective-permute-done.2 = f32[6,1,130]{2,1,0:T(1,128)S(1)} collective-permute-done((f32[6,1,130]{2,1,0:T(1,128)S(1)}, f32[6,1,130]{2,1,0:T(1,128)S(1)}, u32[]{:S(2)}, u32[]{:S(2)}) %collective-permute-start.2) | collective-permute-done | bytes 3152 | tf_op jit(solution)/shard_map/ppermute | solution.py:20
  35.5 3.0 collective-permute-start.5
  40.4 1.9 collective-permute-start.7
  42.3 3.9 %collective-permute-start.6 = (f32[6,1,130]{2,1,0:T(1,128)S(1)}, f32[6,1,130]{2,1,0:T(1,128)S(1)}, u32[]{:S(2)}, u32[]{:S(2)}) collective-permute-start(f32[6,1,130]{2,1,0:T(1,128)S(1)} %get-tuple-element.23), channel_id=1, source_target_pairs={{0,16},{16,32},{32,48},{48,64},{64,80},{80,96},{96,112},{1,17},{17... | collective-permute-start | bytes 9368 | tf_op jit(solution)/shard_map/ppermute | solution.py:20
  46.5 3.5 %collective-permute-done.6 = f32[6,1,130]{2,1,0:T(1,128)S(1)} collective-permute-done((f32[6,1,130]{2,1,0:T(1,128)S(1)}, f32[6,1,130]{2,1,0:T(1,128)S(1)}, u32[]{:S(2)}, u32[]{:S(2)}) %collective-permute-start.6) | collective-permute-done | bytes 3152 | tf_op jit(solution)/shard_map/ppermute | solution.py:20
  56.4 11.9 %concatenate.120 = f32[54,2048]{1,0:T(8,128)} concatenate(f32[6,2048]{1,0:T(8,128)S(1)} %broadcast.26, f32[6,2048]{1,0:T(8,128)S(1)} %bitcast_multiply_fusion.2, f32[6,2048]{1,0:T(8,128)S(1)} %broadcast.26, f32[6,2048]{1,0:T(8,128)S(1)} %bitcast_multiply_fusion.2, f32[6,2048]{1,0:T(8,128)} %fusion.13, f32[6,2048]{1,0:T(8,128)S(1)} %bitcast_multiply_fusion.2, ...), dimensions={0} | concatenate | bytes 884736 | tf_op jit(solution)/shard_map/concatenate | solution.py:112
  70.0 2.9 collective-permute-start.9
  74.0 5.0 %collective-permute-done.8 = f32[54,16,1]{2,1,0:T(8,128)S(1)} collective-permute-done((f32[54,16,1]{2,1,0:T(8,128)S(1)}, f32[54,16,1]{2,1,0:T(8,128)S(1)}, u32[]{:S(2)}, u32[]{:S(2)}) %collective-permute-start.8) | collective-permute-done | bytes 3488 | tf_op jit(solution)/shard_map/ppermute | solution.py:20
  80.0 2.0 collective-permute-start.10
  82.1 4.1 %collective-permute-start.11 = (f32[54,1,130]{2,1,0:T(1,128)}, f32[54,1,130]{2,1,0:T(1,128)}, u32[]{:S(2)}, u32[]{:S(2)}) collective-permute-start(f32[54,1,130]{2,1,0:T(1,128)} %get-tuple-element.15), channel_id=1, source_target_pairs={{0,16},{16,32},{32,48},{48,64},{64,80},{80,96},{96,112},{1,17},{17... | collective-permute-start | bytes 84248 | tf_op jit(solution)/shard_map/ppermute | solution.py:20
  86.5 4.2 %collective-permute-done.11 = f32[54,1,130]{2,1,0:T(1,128)} collective-permute-done((f32[54,1,130]{2,1,0:T(1,128)}, f32[54,1,130]{2,1,0:T(1,128)}, u32[]{:S(2)}, u32[]{:S(2)}) %collective-permute-start.11) | collective-permute-done | bytes 28112 | tf_op jit(solution)/shard_map/ppermute | solution.py:20
  95.1 2.9 collective-permute-start.13
  98.8 5.3 %collective-permute-done.12 = f32[54,16,1]{2,1,0:T(8,128)S(1)} collective-permute-done((f32[54,16,1]{2,1,0:T(8,128)S(1)}, f32[54,16,1]{2,1,0:T(8,128)S(1)}, u32[]{:S(2)}, u32[]{:S(2)}) %collective-permute-start.12) | collective-permute-done | bytes 3488 | tf_op jit(solution)/shard_map/ppermute | solution.py:20
  104.5 1.9 collective-permute-start.14
  106.4 3.9 %collective-permute-start.15 = (f32[54,1,130]{2,1,0:T(1,128)S(1)}, f32[54,1,130]{2,1,0:T(1,128)S(1)}, u32[]{:S(2)}, u32[]{:S(2)}) collective-permute-start(f32[54,1,130]{2,1,0:T(1,128)S(1)} %get-tuple-element.13), channel_id=1, source_target_pairs={{0,16},{16,32},{32,48},{48,64},{64,80},{80,96},{96,112},{1,17},{17... | collective-permute-start | bytes 84248 | tf_op jit(solution)/shard_map/ppermute | solution.py:20
  110.3 93.3 %all-reduce.3.cloned.1.call-done = f32[24064]{0:T(1024)} async-done(((f32[24064]{0:T(1024)}), f32[24064]{0:T(1024)}) %all-reduce.3.cloned.1.call-update) | async-done | bytes 96272 | tf_op jit(solution)/shard_map/psum | solution.py:169
  206.8 20.1 %psum.23 = f32[]{:T(128)} all-reduce(f32[]{:T(128)} %multiply_reduce_fusion), channel_id=1, replica_groups=mesh['ens'=4,'lat'=8,'lon'=16] {'lat'}, use_global_device_ids=true, to_apply=%region_4.0 | all-reduce | flops 1 | bytes 8 | tf_op jit(solution)/shard_map/psum | solution.py:170
  226.9 64.6 %all-reduce.5.cloned.1.call-done = f32[24064]{0:T(1024)} async-done(((f32[24064]{0:T(1024)}), f32[24064]{0:T(1024)}) %all-reduce.5.cloned.1.call-update) | async-done | bytes 96272 | tf_op jit(solution)/shard_map/psum | solution.py:170
  291.5 1.5 multiply_reduce_fusion.1
  295.1 1.6 subtract_add_fusion
  (135 shorter events, 26.8 us)
Async XLA Ops:
  7.2 18.8 %copy-start = (f32[6,6]{1,0:T(8,128)S(1)}, f32[6,6]{1,0:T(8,128)}, u32[]{:S(2)}) copy-start(f32[6,6]{1,0:T(8,128)} %param.11) | copy-start | bytes 436
  7.2 11.3 %copy-start.1 = (f32[6,16,128]{2,1,0:T(8,128)S(1)}, f32[6,16,128]{2,1,0:T(8,128)}, u32[]{:S(2)}) copy-start(f32[6,16,128]{2,1,0:T(8,128)} %param.9) | copy-start | bytes 147460
  7.2 196.4 %all-reduce.3.cloned.1.call-start = ((), (), s32[]{:S(2)}) async-start(), calls=%async_computation | async-start | bytes 196608 | tf_op jit(solution)/shard_map/psum | solution.py:169
  8.2 10.3 %collective-permute-start = (f32[6,16,1]{2,1,0:T(8,128)S(1)}, f32[6,16,1]{2,1,0:T(8,128)S(1)}, u32[]{:S(2)}, u32[]{:S(2)}) collective-permute-start(f32[6,16,1]{2,1,0:T(8,128)S(1)} %get-tuple-element.30), channel_id=1, source_target_pairs={{0,1},{1,2},{2,3},{3,4},{4,5},{5,6},{6,7},{7,8},{8,9},{9,10},{10,1... | collective-permute-start | bytes 1160 | tf_op jit(solution)/shard_map/ppermute | solution.py:20
  8.2 10.2 %collective-permute-start.1 = (f32[6,16,1]{2,1,0:T(8,128)S(1)}, f32[6,16,1]{2,1,0:T(8,128)S(1)}, u32[]{:S(2)}, u32[]{:S(2)}) collective-permute-start(f32[6,16,1]{2,1,0:T(8,128)S(1)} %get-tuple-element.31), channel_id=1, source_target_pairs={{1,0},{2,1},{3,2},{4,3},{5,4},{6,5},{7,6},{8,7},{9,8},{10,9},{11,1... | collective-permute-start | bytes 1160 | tf_op jit(solution)/shard_map/ppermute | solution.py:21
  18.6 8.1 %collective-permute-start.3 = (f32[6,1,130]{2,1,0:T(1,128)S(1)}, f32[6,1,130]{2,1,0:T(1,128)S(1)}, u32[]{:S(2)}, u32[]{:S(2)}) collective-permute-start(f32[6,1,130]{2,1,0:T(1,128)S(1)} %get-tuple-element.26), channel_id=1, source_target_pairs={{16,0},{32,16},{48,32},{64,48},{80,64},{96,80},{112,96},{17,1},{33... | collective-permute-start | bytes 9368 | tf_op jit(solution)/shard_map/ppermute | solution.py:21
  24.0 7.6 %collective-permute-start.2 = (f32[6,1,130]{2,1,0:T(1,128)S(1)}, f32[6,1,130]{2,1,0:T(1,128)S(1)}, u32[]{:S(2)}, u32[]{:S(2)}) collective-permute-start(f32[6,1,130]{2,1,0:T(1,128)S(1)} %get-tuple-element.27), channel_id=1, source_target_pairs={{0,16},{16,32},{32,48},{48,64},{64,80},{80,96},{96,112},{1,17},{17... | collective-permute-start | bytes 9368 | tf_op jit(solution)/shard_map/ppermute | solution.py:20
  26.7 25.1 %copy-start.14 = (f32[16,128]{1,0:T(8,128)}, f32[16,128]{1,0:T(8,128)S(1)}, u32[]{:S(2)}) copy-start(f32[16,128]{1,0:T(8,128)S(1)} %convert_element_type.70) | copy-start | bytes 24580
  35.5 4.7 %collective-permute-start.4 = (f32[6,16,1]{2,1,0:T(8,128)S(1)}, f32[6,16,1]{2,1,0:T(8,128)S(1)}, u32[]{:S(2)}, u32[]{:S(2)}) collective-permute-start(f32[6,16,1]{2,1,0:T(8,128)S(1)} %get-tuple-element.28), channel_id=1, source_target_pairs={{0,1},{1,2},{2,3},{3,4},{4,5},{5,6},{6,7},{7,8},{8,9},{9,10},{10,1... | collective-permute-start | bytes 1160 | tf_op jit(solution)/shard_map/ppermute | solution.py:20
  35.5 4.7 %collective-permute-start.5 = (f32[6,16,1]{2,1,0:T(8,128)S(1)}, f32[6,16,1]{2,1,0:T(8,128)S(1)}, u32[]{:S(2)}, u32[]{:S(2)}) collective-permute-start(f32[6,16,1]{2,1,0:T(8,128)S(1)} %get-tuple-element.29), channel_id=1, source_target_pairs={{1,0},{2,1},{3,2},{4,3},{5,4},{6,5},{7,6},{8,7},{9,8},{10,9},{11,1... | collective-permute-start | bytes 1160 | tf_op jit(solution)/shard_map/ppermute | solution.py:21
  40.4 6.1 %collective-permute-start.7 = (f32[6,1,130]{2,1,0:T(1,128)S(1)}, f32[6,1,130]{2,1,0:T(1,128)S(1)}, u32[]{:S(2)}, u32[]{:S(2)}) collective-permute-start(f32[6,1,130]{2,1,0:T(1,128)S(1)} %get-tuple-element.22), channel_id=1, source_target_pairs={{16,0},{32,16},{48,32},{64,48},{80,64},{96,80},{112,96},{17,1},{33... | collective-permute-start | bytes 9368 | tf_op jit(solution)/shard_map/ppermute | solution.py:21
  42.3 7.6 %collective-permute-start.6 = (f32[6,1,130]{2,1,0:T(1,128)S(1)}, f32[6,1,130]{2,1,0:T(1,128)S(1)}, u32[]{:S(2)}, u32[]{:S(2)}) collective-permute-start(f32[6,1,130]{2,1,0:T(1,128)S(1)} %get-tuple-element.23), channel_id=1, source_target_pairs={{0,16},{16,32},{32,48},{48,64},{64,80},{80,96},{96,112},{1,17},{17... | collective-permute-start | bytes 9368 | tf_op jit(solution)/shard_map/ppermute | solution.py:20
  70.0 8.9 %collective-permute-start.8 = (f32[54,16,1]{2,1,0:T(8,128)S(1)}, f32[54,16,1]{2,1,0:T(8,128)S(1)}, u32[]{:S(2)}, u32[]{:S(2)}) collective-permute-start(f32[54,16,1]{2,1,0:T(8,128)S(1)} %get-tuple-element.18), channel_id=1, source_target_pairs={{0,1},{1,2},{2,3},{3,4},{4,5},{5,6},{6,7},{7,8},{8,9},{9,10},{10,1... | collective-permute-start | bytes 10376 | tf_op jit(solution)/shard_map/ppermute | solution.py:20
  70.0 8.9 %collective-permute-start.9 = (f32[54,16,1]{2,1,0:T(8,128)S(1)}, f32[54,16,1]{2,1,0:T(8,128)S(1)}, u32[]{:S(2)}, u32[]{:S(2)}) collective-permute-start(f32[54,16,1]{2,1,0:T(8,128)S(1)} %get-tuple-element.19), channel_id=1, source_target_pairs={{1,0},{2,1},{3,2},{4,3},{5,4},{6,5},{7,6},{8,7},{9,8},{10,9},{11,1... | collective-permute-start | bytes 10376 | tf_op jit(solution)/shard_map/ppermute | solution.py:21
  74.0 12.2 %copy-start.5 = (f32[1,6,16,128]{3,2,1,0:T(8,128)S(1)}, f32[1,6,16,128]{3,2,1,0:T(8,128)}, u32[]{:S(2)}) copy-start(f32[1,6,16,128]{3,2,1,0:T(8,128)} %copy-done.4) | copy-start | bytes 147460
  80.0 6.5 %collective-permute-start.10 = (f32[54,1,130]{2,1,0:T(1,128)}, f32[54,1,130]{2,1,0:T(1,128)S(1)}, u32[]{:S(2)}, u32[]{:S(2)}) collective-permute-start(f32[54,1,130]{2,1,0:T(1,128)} %get-tuple-element.14), channel_id=1, source_target_pairs={{16,0},{32,16},{48,32},{64,48},{80,64},{96,80},{112,96},{17,1},{33... | collective-permute-start | bytes 84248 | tf_op jit(solution)/shard_map/ppermute | solution.py:21
  82.1 8.6 %collective-permute-start.11 = (f32[54,1,130]{2,1,0:T(1,128)}, f32[54,1,130]{2,1,0:T(1,128)}, u32[]{:S(2)}, u32[]{:S(2)}) collective-permute-start(f32[54,1,130]{2,1,0:T(1,128)} %get-tuple-element.15), channel_id=1, source_target_pairs={{0,16},{16,32},{32,48},{48,64},{64,80},{80,96},{96,112},{1,17},{17... | collective-permute-start | bytes 84248 | tf_op jit(solution)/shard_map/ppermute | solution.py:20
  95.1 8.9 %collective-permute-start.12 = (f32[54,16,1]{2,1,0:T(8,128)S(1)}, f32[54,16,1]{2,1,0:T(8,128)S(1)}, u32[]{:S(2)}, u32[]{:S(2)}) collective-permute-start(f32[54,16,1]{2,1,0:T(8,128)S(1)} %get-tuple-element.16), channel_id=1, source_target_pairs={{0,1},{1,2},{2,3},{3,4},{4,5},{5,6},{6,7},{7,8},{8,9},{9,10},{10,1... | collective-permute-start | bytes 10376 | tf_op jit(solution)/shard_map/ppermute | solution.py:20
  95.1 8.9 %collective-permute-start.13 = (f32[54,16,1]{2,1,0:T(8,128)S(1)}, f32[54,16,1]{2,1,0:T(8,128)S(1)}, u32[]{:S(2)}, u32[]{:S(2)}) collective-permute-start(f32[54,16,1]{2,1,0:T(8,128)S(1)} %get-tuple-element.17), channel_id=1, source_target_pairs={{1,0},{2,1},{3,2},{4,3},{5,4},{6,5},{7,6},{8,7},{9,8},{10,9},{11,1... | collective-permute-start | bytes 10376 | tf_op jit(solution)/shard_map/ppermute | solution.py:21
  104.5 101.4 %collective-permute-start.14 = (f32[54,1,130]{2,1,0:T(1,128)S(1)}, f32[54,1,130]{2,1,0:T(1,128)S(1)}, u32[]{:S(2)}, u32[]{:S(2)}) collective-permute-start(f32[54,1,130]{2,1,0:T(1,128)S(1)} %get-tuple-element.12), channel_id=1, source_target_pairs={{16,0},{32,16},{48,32},{64,48},{80,64},{96,80},{112,96},{17,1},{33... | collective-permute-start | bytes 84248 | tf_op jit(solution)/shard_map/ppermute | solution.py:21
  106.4 99.5 %collective-permute-start.15 = (f32[54,1,130]{2,1,0:T(1,128)S(1)}, f32[54,1,130]{2,1,0:T(1,128)S(1)}, u32[]{:S(2)}, u32[]{:S(2)}) collective-permute-start(f32[54,1,130]{2,1,0:T(1,128)S(1)} %get-tuple-element.13), channel_id=1, source_target_pairs={{0,16},{16,32},{32,48},{48,64},{64,80},{80,96},{96,112},{1,17},{17... | collective-permute-start | bytes 84248 | tf_op jit(solution)/shard_map/ppermute | solution.py:20
  205.1 86.4 %all-reduce.5.cloned.1.call-start = ((), (), s32[]{:S(2)}) async-start(), calls=%async_computation.1 | async-start | bytes 196608 | tf_op jit(solution)/shard_map/psum | solution.py:170
  205.9 89.2 %copy-start.16 = (f32[24064]{0:T(1024)S(1)}, f32[24064]{0:T(1024)}, u32[]{:S(2)}) copy-start(f32[24064]{0:T(1024)} %param.17) | copy-start | bytes 288772
  226.9 68.2 %copy-start.8 = (bf16[128,128]{1,0:T(8,128)(2,1)S(1)}, bf16[128,128]{1,0:T(8,128)(2,1)}, u32[]{:S(2)}) copy-start(bf16[128,128]{1,0:T(8,128)(2,1)} %param.14) | copy-start | bytes 98308
  (15 other events, 34.2 us)
Sparse Core Ops, SparseCore 0:
  98.9 104.6 all-reduce.2
  209.1 82.3 all-reduce.4
where the time goes:
time: 306 us; the launch traced here: 305 us
  waiting for transfers between devices  184 us (60%)
  starting transfers between devices  42.6 us (14%)
  local copies, waits for them, and re-layouts  20.1 us (7%)
  blocking collectives  20.1 us (7%)
  between operations  17.7 us (6%)
  other arithmetic  10.5 us (3%)
  matrix products  9.52 us (3%)
    psum x1, waiting for transfers between devices, on_device(): band = lax.psum(local_grad, 'lon')  93.3 us
    psum x1, waiting for transfers between devices, on_device(): total_grad, band_square = lax.psum((band, jnp.sum(band * band)), 'lat')  64.6 us
    ppermute x8, starting transfers between devices, with_halo(): after = lax.ppermute(first, axis, down)  28.7 us
    ppermute x8, waiting for transfers between devices, with_halo(): before = lax.ppermute(last, axis, up)  25.5 us
    psum x1, blocking collectives, on_device(): total_grad, band_square = lax.psum((band, jnp.sum(band * band)), 'lat')  20.1 us
    ppermute x8, starting transfers between devices, with_halo(): before = lax.ppermute(last, axis, up)  13.9 us
    concatenate x2, local copies, waits for them, and re-layouts, backward_block(): jnp.concatenate([blank, spread, blank, spread, direct - 4.0 * spread, spr...  12.4 us
  transfers between devices with their start and end apart: 18, of which 9 were waited for; matrix products, arithmetic and copies ran while one was open for 2% of the time, Pallas kernels for 0%

commit v1 on v0

--- a/solution.py
+++ b/solution.py
@@ -166,7 +166,9 @@
             )
         adjoint = total
     params_count = local_grad.shape[0]
-    band = lax.psum(local_grad, "lon")
+    band = local_grad
+    for hop in (1, 2, 4, 8):
+        band = band + lax.ppermute(band, "lon", [(dev, dev ^ hop) for dev in range(16)])
     total_grad, band_square = lax.psum((band, jnp.sum(band * band)), "lat")
     grad_square = jnp.sum(total_grad * total_grad)
     noise_ratio = (band_square / (grad_square + epsilon)).reshape(1)

time: 306 us -> 221 us (0.72)
  waiting for transfers between devices: 184 us -> 91.7 us
  starting transfers between devices: 42.6 us -> 54.2 us
  blocking collectives: 20.1 us -> 16.6 us
    psum x1 -> x0, waiting for transfers between devices: 93.3 us -> none  [on_device(): band = lax.psum(local_grad, 'lon')]
    ppermute x0 -> x4, starting transfers between devices: none -> 11.6 us  [on_device(): lax.ppermute(band, 'lon', [(dev, dev ^ hop) for dev in range(16)])]
    ppermute x0 -> x4, waiting for transfers between devices: none -> 9.5 us  [on_device(): lax.ppermute(band, 'lon', [(dev, dev ^ hop) for dev in range(16)])]
    psum x1, waiting for transfers between devices: 64.6 us -> 59.1 us  [on_device(): total_grad, band_square = lax.psum((band, jnp.sum(band * band)), 'lat')]
    psum x1, blocking collectives: 20.1 us -> 16.6 us  [on_device(): total_grad, band_square = lax.psum((band, jnp.sum(band * band)), 'lat')]
  transfers between devices with their start and end apart: 18 -> 21, of which waited for: 9 -> 12; matrix products, arithmetic and copies ran while one was open for 2% -> 3% of each run, Pallas kernels for 0% -> 0%
where the time goes in v1:
time: 221 us; the launch traced here: 219 us
  waiting for transfers between devices  91.7 us (41%)
  starting transfers between devices  54.2 us (25%)
  local copies, waits for them, and re-layouts  20.7 us (9%)
  between operations  17.7 us (8%)
  blocking collectives  16.6 us (8%)
  matrix products  9.54 us (4%)
  other arithmetic  8.75 us (4%)
    psum x1, waiting for transfers between devices, on_device(): total_grad, band_square = lax.psum((band, jnp.sum(band * band)), 'lat')  59.1 us
    ppermute x8, starting transfers between devices, with_halo(): after = lax.ppermute(first, axis, down)  28.3 us
    ppermute x8, waiting for transfers between devices, with_halo(): before = lax.ppermute(last, axis, up)  23.1 us
    psum x1, blocking collectives, on_device(): total_grad, band_square = lax.psum((band, jnp.sum(band * band)), 'lat')  16.6 us
    ppermute x8, starting transfers between devices, with_halo(): before = lax.ppermute(last, axis, up)  14.2 us
    concatenate x2, local copies, waits for them, and re-layouts, backward_block(): jnp.concatenate([blank, spread, blank, spread, direct - 4.0 * spread, spr...  12.5 us
    ppermute x4, starting transfers between devices, on_device(): lax.ppermute(band, 'lon', [(dev, dev ^ hop) for dev in range(16)])  11.6 us
    ppermute x4, waiting for transfers between devices, on_device(): lax.ppermute(band, 'lon', [(dev, dev ^ hop) for dev in range(16)])  9.5 us
  transfers between devices with their start and end apart: 21, of which 12 were waited for; matrix products, arithmetic and copies ran while one was open for 3% of the time, Pallas kernels for 0%

profile of v1, /device:TPU:40, one launch (start us, length us, event | category | flops | bytes accessed | tf_op | source)
XLA Modules:
  0.0 219.3 jit_solution(8801766002592100456)
XLA Ops:
  8.2 8.5 %collective-permute-start.1 = (f32[6,16,1]{2,1,0:T(8,128)S(1)}, f32[6,16,1]{2,1,0:T(8,128)S(1)}, u32[]{:S(2)}, u32[]{:S(2)}) collective-permute-start(f32[6,16,1]{2,1,0:T(8,128)S(1)} %get-tuple-element.33), channel_id=1, source_target_pairs={{1,0},{2,1},{3,2},{4,3},{5,4},{6,5},{7,6},{8,7},{9,8},{10,9},{11,1... | collective-permute-start | bytes 1160 | tf_op jit(solution)/shard_map/ppermute | solution.py:21
  18.6 5.5 %collective-permute-start.3 = (f32[6,1,130]{2,1,0:T(1,128)S(1)}, f32[6,1,130]{2,1,0:T(1,128)S(1)}, u32[]{:S(2)}, u32[]{:S(2)}) collective-permute-start(f32[6,1,130]{2,1,0:T(1,128)S(1)} %get-tuple-element.28), channel_id=1, source_target_pairs={{16,0},{32,16},{48,32},{64,48},{80,64},{96,80},{112,96},{17,1},{33... | collective-permute-start | bytes 9368 | tf_op jit(solution)/shard_map/ppermute | solution.py:21
  24.0 1.9 collective-permute-start.2
  26.7 5.0 %collective-permute-done.2 = f32[6,1,130]{2,1,0:T(1,128)S(1)} collective-permute-done((f32[6,1,130]{2,1,0:T(1,128)S(1)}, f32[6,1,130]{2,1,0:T(1,128)S(1)}, u32[]{:S(2)}, u32[]{:S(2)}) %collective-permute-start.2) | collective-permute-done | bytes 3152 | tf_op jit(solution)/shard_map/ppermute | solution.py:20
  35.5 3.0 %collective-permute-start.5 = (f32[6,16,1]{2,1,0:T(8,128)S(1)}, f32[6,16,1]{2,1,0:T(8,128)S(1)}, u32[]{:S(2)}, u32[]{:S(2)}) collective-permute-start(f32[6,16,1]{2,1,0:T(8,128)S(1)} %get-tuple-element.31), channel_id=1, source_target_pairs={{1,0},{2,1},{3,2},{4,3},{5,4},{6,5},{7,6},{8,7},{9,8},{10,9},{11,1... | collective-permute-start | bytes 1160 | tf_op jit(solution)/shard_map/ppermute | solution.py:21
  40.4 1.9 collective-permute-start.7
  42.3 3.9 %collective-permute-start.6 = (f32[6,1,130]{2,1,0:T(1,128)S(1)}, f32[6,1,130]{2,1,0:T(1,128)S(1)}, u32[]{:S(2)}, u32[]{:S(2)}) collective-permute-start(f32[6,1,130]{2,1,0:T(1,128)S(1)} %get-tuple-element.25), channel_id=1, source_target_pairs={{0,16},{16,32},{32,48},{48,64},{64,80},{80,96},{96,112},{1,17},{17... | collective-permute-start | bytes 9368 | tf_op jit(solution)/shard_map/ppermute | solution.py:20
  46.5 3.5 %collective-permute-done.6 = f32[6,1,130]{2,1,0:T(1,128)S(1)} collective-permute-done((f32[6,1,130]{2,1,0:T(1,128)S(1)}, f32[6,1,130]{2,1,0:T(1,128)S(1)}, u32[]{:S(2)}, u32[]{:S(2)}) %collective-permute-start.6) | collective-permute-done | bytes 3152 | tf_op jit(solution)/shard_map/ppermute | solution.py:20
  56.4 11.9 %concatenate.120 = f32[54,2048]{1,0:T(8,128)} concatenate(f32[6,2048]{1,0:T(8,128)S(1)} %broadcast.26, f32[6,2048]{1,0:T(8,128)S(1)} %bitcast_multiply_fusion.2, f32[6,2048]{1,0:T(8,128)S(1)} %broadcast.26, f32[6,2048]{1,0:T(8,128)S(1)} %bitcast_multiply_fusion.2, f32[6,2048]{1,0:T(8,128)} %fusion.13, f32[6,2048]{1,0:T(8,128)S(1)} %bitcast_multiply_fusion.2, ...), dimensions={0} | concatenate | bytes 884736 | tf_op jit(solution)/shard_map/concatenate | solution.py:112
  70.1 2.9 %collective-permute-start.9 = (f32[54,16,1]{2,1,0:T(8,128)S(1)}, f32[54,16,1]{2,1,0:T(8,128)S(1)}, u32[]{:S(2)}, u32[]{:S(2)}) collective-permute-start(f32[54,16,1]{2,1,0:T(8,128)S(1)} %get-tuple-element.21), channel_id=1, source_target_pairs={{1,0},{2,1},{3,2},{4,3},{5,4},{6,5},{7,6},{8,7},{9,8},{10,9},{11,1... | collective-permute-start | bytes 10376 | tf_op jit(solution)/shard_map/ppermute | solution.py:21
  74.1 5.0 %collective-permute-done.8 = f32[54,16,1]{2,1,0:T(8,128)S(1)} collective-permute-done((f32[54,16,1]{2,1,0:T(8,128)S(1)}, f32[54,16,1]{2,1,0:T(8,128)S(1)}, u32[]{:S(2)}, u32[]{:S(2)}) %collective-permute-start.8) | collective-permute-done | bytes 3488 | tf_op jit(solution)/shard_map/ppermute | solution.py:20
  80.1 2.0 collective-permute-start.10
  82.2 4.1 %collective-permute-start.11 = (f32[54,1,130]{2,1,0:T(1,128)}, f32[54,1,130]{2,1,0:T(1,128)}, u32[]{:S(2)}, u32[]{:S(2)}) collective-permute-start(f32[54,1,130]{2,1,0:T(1,128)} %get-tuple-element.17), channel_id=1, source_target_pairs={{0,16},{16,32},{32,48},{48,64},{64,80},{80,96},{96,112},{1,17},{17... | collective-permute-start | bytes 84248 | tf_op jit(solution)/shard_map/ppermute | solution.py:20
  86.6 4.2 %collective-permute-done.11 = f32[54,1,130]{2,1,0:T(1,128)} collective-permute-done((f32[54,1,130]{2,1,0:T(1,128)}, f32[54,1,130]{2,1,0:T(1,128)}, u32[]{:S(2)}, u32[]{:S(2)}) %collective-permute-start.11) | collective-permute-done | bytes 28112 | tf_op jit(solution)/shard_map/ppermute | solution.py:20
  94.5 1.9 collective-permute-start.16
  97.7 1.9 collective-permute-start.17
  100.2 2.6 %collective-permute-start.13 = (f32[54,16,1]{2,1,0:T(8,128)S(1)}, f32[54,16,1]{2,1,0:T(8,128)S(1)}, u32[]{:S(2)}, u32[]{:S(2)}) collective-permute-start(f32[54,16,1]{2,1,0:T(8,128)S(1)} %get-tuple-element.19), channel_id=1, source_target_pairs={{1,0},{2,1},{3,2},{4,3},{5,4},{6,5},{7,6},{8,7},{9,8},{10,9},{11,1... | collective-permute-start | bytes 10376 | tf_op jit(solution)/shard_map/ppermute | solution.py:21
  104.7 3.4 %collective-permute-start.18 = (f32[24064]{0:T(1024)S(1)}, f32[24064]{0:T(1024)S(1)}, u32[]{:S(2)}, u32[]{:S(2)}) collective-permute-start(f32[24064]{0:T(1024)S(1)} %add.162), channel_id=1, source_target_pairs={{0,4},{1,5},{2,6},{3,7},{4,0},{5,1},{6,2},{7,3},{8,12},{9,13},{10,... | collective-permute-start | bytes 288776 | tf_op jit(solution)/shard_map/ppermute | solution.py:171
  108.2 7.3 %collective-permute-done.18 = f32[24064]{0:T(1024)S(1)} collective-permute-done((f32[24064]{0:T(1024)S(1)}, f32[24064]{0:T(1024)S(1)}, u32[]{:S(2)}, u32[]{:S(2)}) %collective-permute-start.18) | collective-permute-done | bytes 96288 | tf_op jit(solution)/shard_map/ppermute | solution.py:171
  115.5 4.4 %collective-permute-start.19 = (f32[24064]{0:T(1024)S(1)}, f32[24064]{0:T(1024)S(1)}, u32[]{:S(2)}, u32[]{:S(2)}) collective-permute-start(f32[24064]{0:T(1024)S(1)} %add.163), channel_id=1, source_target_pairs={{0,8},{1,9},{2,10},{3,11},{4,12},{5,13},{6,14},{7,15},{8,0},{9,1},... | collective-permute-start | bytes 288776 | tf_op jit(solution)/shard_map/ppermute | solution.py:171
  122.2 3.9 %collective-permute-start.15 = (f32[54,1,130]{2,1,0:T(1,128)S(1)}, f32[54,1,130]{2,1,0:T(1,128)S(1)}, u32[]{:S(2)}, u32[]{:S(2)}) collective-permute-start(f32[54,1,130]{2,1,0:T(1,128)S(1)} %get-tuple-element.15), channel_id=1, source_target_pairs={{0,16},{16,32},{32,48},{48,64},{64,80},{80,96},{96,112},{1,17},{17... | collective-permute-start | bytes 84248 | tf_op jit(solution)/shard_map/ppermute | solution.py:20
  127.6 2.8 %collective-permute-done.15 = f32[54,1,130]{2,1,0:T(1,128)S(1)} collective-permute-done((f32[54,1,130]{2,1,0:T(1,128)S(1)}, f32[54,1,130]{2,1,0:T(1,128)S(1)}, u32[]{:S(2)}, u32[]{:S(2)}) %collective-permute-start.15) | collective-permute-done | bytes 28112 | tf_op jit(solution)/shard_map/ppermute | solution.py:20
  131.3 16.6 %psum.15 = f32[]{:T(128)} all-reduce(f32[]{:T(128)} %get-tuple-element.4), channel_id=1, replica_groups=mesh['ens'=4,'lat'=8,'lon'=16] {'lat'}, use_global_device_ids=true, to_apply=%region_3.0 | all-reduce | flops 1 | bytes 8 | tf_op jit(solution)/shard_map/psum | solution.py:172
  147.9 59.1 %all-reduce.2.cloned.1.call-done = f32[24064]{0:T(1024)} async-done(((f32[24064]{0:T(1024)}), f32[24064]{0:T(1024)}) %all-reduce.2.cloned.1.call-update) | async-done | bytes 96272 | tf_op jit(solution)/shard_map/psum | solution.py:172
  (143 shorter events, 34.3 us)
Async XLA Ops:
  7.2 199.9 %all-reduce.2.cloned.1.call-start = ((), (), s32[]{:S(2)}) async-start(), calls=%async_computation | async-start | bytes 196608 | tf_op jit(solution)/shard_map/psum | solution.py:172
  8.2 10.3 %collective-permute-start = (f32[6,16,1]{2,1,0:T(8,128)S(1)}, f32[6,16,1]{2,1,0:T(8,128)S(1)}, u32[]{:S(2)}, u32[]{:S(2)}) collective-permute-start(f32[6,16,1]{2,1,0:T(8,128)S(1)} %get-tuple-element.32), channel_id=1, source_target_pairs={{0,1},{1,2},{2,3},{3,4},{4,5},{5,6},{6,7},{7,8},{8,9},{9,10},{10,1... | collective-permute-start | bytes 1160 | tf_op jit(solution)/shard_map/ppermute | solution.py:20
  8.2 10.2 %collective-permute-start.1 = (f32[6,16,1]{2,1,0:T(8,128)S(1)}, f32[6,16,1]{2,1,0:T(8,128)S(1)}, u32[]{:S(2)}, u32[]{:S(2)}) collective-permute-start(f32[6,16,1]{2,1,0:T(8,128)S(1)} %get-tuple-element.33), channel_id=1, source_target_pairs={{1,0},{2,1},{3,2},{4,3},{5,4},{6,5},{7,6},{8,7},{9,8},{10,9},{11,1... | collective-permute-start | bytes 1160 | tf_op jit(solution)/shard_map/ppermute | solution.py:21
  18.6 8.1 %collective-permute-start.3 = (f32[6,1,130]{2,1,0:T(1,128)S(1)}, f32[6,1,130]{2,1,0:T(1,128)S(1)}, u32[]{:S(2)}, u32[]{:S(2)}) collective-permute-start(f32[6,1,130]{2,1,0:T(1,128)S(1)} %get-tuple-element.28), channel_id=1, source_target_pairs={{16,0},{32,16},{48,32},{64,48},{80,64},{96,80},{112,96},{17,1},{33... | collective-permute-start | bytes 9368 | tf_op jit(solution)/shard_map/ppermute | solution.py:21
  24.0 7.6 %collective-permute-start.2 = (f32[6,1,130]{2,1,0:T(1,128)S(1)}, f32[6,1,130]{2,1,0:T(1,128)S(1)}, u32[]{:S(2)}, u32[]{:S(2)}) collective-permute-start(f32[6,1,130]{2,1,0:T(1,128)S(1)} %get-tuple-element.29), channel_id=1, source_target_pairs={{0,16},{16,32},{32,48},{48,64},{64,80},{80,96},{96,112},{1,17},{17... | collective-permute-start | bytes 9368 | tf_op jit(solution)/shard_map/ppermute | solution.py:20
  26.7 25.1 %copy-start.14 = (f32[16,128]{1,0:T(8,128)}, f32[16,128]{1,0:T(8,128)S(1)}, u32[]{:S(2)}) copy-start(f32[16,128]{1,0:T(8,128)S(1)} %convert_element_type.70) | copy-start | bytes 24580
  35.5 4.7 %collective-permute-start.4 = (f32[6,16,1]{2,1,0:T(8,128)S(1)}, f32[6,16,1]{2,1,0:T(8,128)S(1)}, u32[]{:S(2)}, u32[]{:S(2)}) collective-permute-start(f32[6,16,1]{2,1,0:T(8,128)S(1)} %get-tuple-element.30), channel_id=1, source_target_pairs={{0,1},{1,2},{2,3},{3,4},{4,5},{5,6},{6,7},{7,8},{8,9},{9,10},{10,1... | collective-permute-start | bytes 1160 | tf_op jit(solution)/shard_map/ppermute | solution.py:20
  35.5 4.7 %collective-permute-start.5 = (f32[6,16,1]{2,1,0:T(8,128)S(1)}, f32[6,16,1]{2,1,0:T(8,128)S(1)}, u32[]{:S(2)}, u32[]{:S(2)}) collective-permute-start(f32[6,16,1]{2,1,0:T(8,128)S(1)} %get-tuple-element.31), channel_id=1, source_target_pairs={{1,0},{2,1},{3,2},{4,3},{5,4},{6,5},{7,6},{8,7},{9,8},{10,9},{11,1... | collective-permute-start | bytes 1160 | tf_op jit(solution)/shard_map/ppermute | solution.py:21
  40.4 6.1 %collective-permute-start.7 = (f32[6,1,130]{2,1,0:T(1,128)S(1)}, f32[6,1,130]{2,1,0:T(1,128)S(1)}, u32[]{:S(2)}, u32[]{:S(2)}) collective-permute-start(f32[6,1,130]{2,1,0:T(1,128)S(1)} %get-tuple-element.24), channel_id=1, source_target_pairs={{16,0},{32,16},{48,32},{64,48},{80,64},{96,80},{112,96},{17,1},{33... | collective-permute-start | bytes 9368 | tf_op jit(solution)/shard_map/ppermute | solution.py:21
  42.3 7.6 %collective-permute-start.6 = (f32[6,1,130]{2,1,0:T(1,128)S(1)}, f32[6,1,130]{2,1,0:T(1,128)S(1)}, u32[]{:S(2)}, u32[]{:S(2)}) collective-permute-start(f32[6,1,130]{2,1,0:T(1,128)S(1)} %get-tuple-element.25), channel_id=1, source_target_pairs={{0,16},{16,32},{32,48},{48,64},{64,80},{80,96},{96,112},{1,17},{17... | collective-permute-start | bytes 9368 | tf_op jit(solution)/shard_map/ppermute | solution.py:20
  70.1 8.9 %collective-permute-start.8 = (f32[54,16,1]{2,1,0:T(8,128)S(1)}, f32[54,16,1]{2,1,0:T(8,128)S(1)}, u32[]{:S(2)}, u32[]{:S(2)}) collective-permute-start(f32[54,16,1]{2,1,0:T(8,128)S(1)} %get-tuple-element.20), channel_id=1, source_target_pairs={{0,1},{1,2},{2,3},{3,4},{4,5},{5,6},{6,7},{7,8},{8,9},{9,10},{10,1... | collective-permute-start | bytes 10376 | tf_op jit(solution)/shard_map/ppermute | solution.py:20
  70.1 8.9 %collective-permute-start.9 = (f32[54,16,1]{2,1,0:T(8,128)S(1)}, f32[54,16,1]{2,1,0:T(8,128)S(1)}, u32[]{:S(2)}, u32[]{:S(2)}) collective-permute-start(f32[54,16,1]{2,1,0:T(8,128)S(1)} %get-tuple-element.21), channel_id=1, source_target_pairs={{1,0},{2,1},{3,2},{4,3},{5,4},{6,5},{7,6},{8,7},{9,8},{10,9},{11,1... | collective-permute-start | bytes 10376 | tf_op jit(solution)/shard_map/ppermute | solution.py:21
  80.1 6.5 %collective-permute-start.10 = (f32[54,1,130]{2,1,0:T(1,128)}, f32[54,1,130]{2,1,0:T(1,128)S(1)}, u32[]{:S(2)}, u32[]{:S(2)}) collective-permute-start(f32[54,1,130]{2,1,0:T(1,128)} %get-tuple-element.16), channel_id=1, source_target_pairs={{16,0},{32,16},{48,32},{64,48},{80,64},{96,80},{112,96},{17,1},{33... | collective-permute-start | bytes 84248 | tf_op jit(solution)/shard_map/ppermute | solution.py:21
  82.2 8.6 %collective-permute-start.11 = (f32[54,1,130]{2,1,0:T(1,128)}, f32[54,1,130]{2,1,0:T(1,128)}, u32[]{:S(2)}, u32[]{:S(2)}) collective-permute-start(f32[54,1,130]{2,1,0:T(1,128)} %get-tuple-element.17), channel_id=1, source_target_pairs={{0,16},{16,32},{32,48},{48,64},{64,80},{80,96},{96,112},{1,17},{17... | collective-permute-start | bytes 84248 | tf_op jit(solution)/shard_map/ppermute | solution.py:20
  94.5 3.2 %collective-permute-start.16 = (f32[24064]{0:T(1024)S(1)}, f32[24064]{0:T(1024)S(1)}, u32[]{:S(2)}, u32[]{:S(2)}) collective-permute-start(f32[24064]{0:T(1024)S(1)} %maximum_add_fusion), channel_id=1, source_target_pairs={{0,1},{1,0},{2,3},{3,2},{4,5},{5,4},{6,7},{7,6},{8,9},{9,8},{10,11... | collective-permute-start | bytes 288776 | tf_op jit(solution)/shard_map/ppermute | solution.py:171
  97.7 7.0 %collective-permute-start.17 = (f32[24064]{0:T(1024)S(1)}, f32[24064]{0:T(1024)S(1)}, u32[]{:S(2)}, u32[]{:S(2)}) collective-permute-start(f32[24064]{0:T(1024)S(1)} %add.161), channel_id=1, source_target_pairs={{0,2},{1,3},{2,0},{3,1},{4,6},{5,7},{6,4},{7,5},{8,10},{9,11},{10,... | collective-permute-start | bytes 288776 | tf_op jit(solution)/shard_map/ppermute | solution.py:171
  99.8 20.0 %collective-permute-start.12 = (f32[54,16,1]{2,1,0:T(8,128)S(1)}, f32[54,16,1]{2,1,0:T(8,128)S(1)}, u32[]{:S(2)}, u32[]{:S(2)}) collective-permute-start(f32[54,16,1]{2,1,0:T(8,128)S(1)} %get-tuple-element.18), channel_id=1, source_target_pairs={{0,1},{1,2},{2,3},{3,4},{4,5},{5,6},{6,7},{7,8},{8,9},{9,10},{10,1... | collective-permute-start | bytes 10376 | tf_op jit(solution)/shard_map/ppermute | solution.py:20
  100.2 19.7 %collective-permute-start.13 = (f32[54,16,1]{2,1,0:T(8,128)S(1)}, f32[54,16,1]{2,1,0:T(8,128)S(1)}, u32[]{:S(2)}, u32[]{:S(2)}) collective-permute-start(f32[54,16,1]{2,1,0:T(8,128)S(1)} %get-tuple-element.19), channel_id=1, source_target_pairs={{1,0},{2,1},{3,2},{4,3},{5,4},{6,5},{7,6},{8,7},{9,8},{10,9},{11,1... | collective-permute-start | bytes 10376 | tf_op jit(solution)/shard_map/ppermute | solution.py:21
  104.7 10.8 %collective-permute-start.18 = (f32[24064]{0:T(1024)S(1)}, f32[24064]{0:T(1024)S(1)}, u32[]{:S(2)}, u32[]{:S(2)}) collective-permute-start(f32[24064]{0:T(1024)S(1)} %add.162), channel_id=1, source_target_pairs={{0,4},{1,5},{2,6},{3,7},{4,0},{5,1},{6,2},{7,3},{8,12},{9,13},{10,... | collective-permute-start | bytes 288776 | tf_op jit(solution)/shard_map/ppermute | solution.py:171
  115.5 10.8 %collective-permute-start.19 = (f32[24064]{0:T(1024)S(1)}, f32[24064]{0:T(1024)S(1)}, u32[]{:S(2)}, u32[]{:S(2)}) collective-permute-start(f32[24064]{0:T(1024)S(1)} %add.163), channel_id=1, source_target_pairs={{0,8},{1,9},{2,10},{3,11},{4,12},{5,13},{6,14},{7,15},{8,0},{9,1},... | collective-permute-start | bytes 288776 | tf_op jit(solution)/shard_map/ppermute | solution.py:171
  120.3 7.3 %collective-permute-start.14 = (f32[54,1,130]{2,1,0:T(1,128)S(1)}, f32[54,1,130]{2,1,0:T(1,128)S(1)}, u32[]{:S(2)}, u32[]{:S(2)}) collective-permute-start(f32[54,1,130]{2,1,0:T(1,128)S(1)} %get-tuple-element.14), channel_id=1, source_target_pairs={{16,0},{32,16},{48,32},{64,48},{80,64},{96,80},{112,96},{17,1},{33... | collective-permute-start | bytes 84248 | tf_op jit(solution)/shard_map/ppermute | solution.py:21
  122.2 8.2 %collective-permute-start.15 = (f32[54,1,130]{2,1,0:T(1,128)S(1)}, f32[54,1,130]{2,1,0:T(1,128)S(1)}, u32[]{:S(2)}, u32[]{:S(2)}) collective-permute-start(f32[54,1,130]{2,1,0:T(1,128)S(1)} %get-tuple-element.15), channel_id=1, source_target_pairs={{0,16},{16,32},{32,48},{48,64},{64,80},{80,96},{96,112},{1,17},{17... | collective-permute-start | bytes 84248 | tf_op jit(solution)/shard_map/ppermute | solution.py:20
  130.4 80.2 %copy-start.16 = (f32[24064]{0:T(1024)S(1)}, f32[24064]{0:T(1024)}, u32[]{:S(2)}) copy-start(f32[24064]{0:T(1024)} %param.17) | copy-start | bytes 288772
  131.3 79.4 %copy-start.17 = (bf16[6912]{0:T(1024)(128)(2,1)S(1)}, bf16[6912]{0:T(1024)(128)(2,1)}, u32[]{:S(2)}) copy-start(bf16[6912]{0:T(1024)(128)(2,1)} %reshape.86) | copy-start | bytes 41476
  (18 other events, 75.9 us)
Sparse Core Ops, SparseCore 0:
  127.7 79.2 all-reduce.1
